TPU v7x, 32 devices: a whole 2x2x4 slice. The times are simulated.
32 devices in a mesh: ctx: 8 (over z, core), tp: 4 (over y, x).
Axes of the slice: x: 2, y: 2, z: 4, core: 2. Of those that a mesh axis runs over, the one named last changes fastest.
Arguments:
- queries: bfloat16 [1024, 8192], P('ctx', 'tp'), may hold values from -6 to 6
- keys_in: bfloat16 [1024, 8192], P('ctx', 'tp'), may hold values from -6 to 6
- values_in: bfloat16 [1024, 8192], P('ctx', 'tp'), may hold values from -6 to 6
- decay_rates: float32 [8192, 16], P('tp'), may hold values from 0.00029296876 to 0.03
- residues: float32 [8192, 16], P('tp'), may hold values from -1.5 to 1.5
- skip_gain: float32 [8192], P('tp'), may hold values from -4 to 4
- cotangent: bfloat16 [1024, 8192], P('ctx', 'tp'), may hold values from -6 to 6
Outputs:
- operator_out: bfloat16 [1024, 8192], P('ctx', 'tp')
- grad_queries: bfloat16 [1024, 8192], P('ctx', 'tp')
- grad_keys: bfloat16 [1024, 8192], P('ctx', 'tp')
- grad_values: bfloat16 [1024, 8192], P('ctx', 'tp')
- grad_residues: float32 [8192, 16], P('tp')
All inputs are finite; a program needn't handle non-finite values.
Results may differ from a plain program's by a relative error of at most 0.0054.
Values may be sent and summed in bfloat16 or wider, within the bound.
No kernel may reach another device: no remote copies, remote signals or barrier semaphores. Data moves between devices by JAX's collectives and lax.ppermute only.
A program may use at most 64 MiB of HBM per device.

v0:
```python
from functools import partial
import math

import jax
import jax.numpy as jnp
from jax import lax
from jax.sharding import PartitionSpec as P

D = 8192
ORDER = 16


PRECISE = lax.Precision.HIGHEST


def chain_link(earlier_pair, later_pair):
    return (earlier_pair[0] * later_pair[0], later_pair[0] * earlier_pair[1] + later_pair[1])


def prepare(decay, weight, block_len):
    positions = jnp.arange(block_len + 1, dtype=jnp.float32)
    powers = jnp.exp(-decay[None] * positions[:, None, None])
    unit_scale = jnp.sqrt(1.0 - jnp.exp(-2.0 * decay))
    mode_coef = weight * unit_scale
    short_filter = jnp.einsum("kcn,cn->kc", powers[:block_len], mode_coef, precision=PRECISE)
    lag_table = jnp.arange(block_len)[:, None] - jnp.arange(block_len)[None, :]
    toeplitz = jnp.where((lag_table >= 0)[:, :, None], short_filter[jnp.maximum(lag_table, 0)], 0.0)
    return (positions, powers, unit_scale, mode_coef, toeplitz, lag_table)


def forward_states(in_blocks, powers, decay, carry_in, block_len):
    block_count = in_blocks.shape[0]
    end_states = jnp.einsum("bsc,scn->bcn", in_blocks, powers[:block_len][::-1], precision=PRECISE)
    decays = jnp.broadcast_to(powers[block_len], end_states.shape)
    _, totals = lax.associative_scan(chain_link, (decays, end_states), axis=0)
    distance = block_len * jnp.arange(1, block_count + 1, dtype=jnp.float32)
    states = totals + jnp.exp(-decay[None] * distance[:, None, None]) * carry_in[None]
    before = jnp.concatenate([carry_in[None], states[:-1]], 0)
    return (before, totals[-1])


def backward_states(back_blocks, powers, decay, carry_back, block_len):
    block_count = back_blocks.shape[0]
    start_states = jnp.einsum("btc,tcn->bcn", back_blocks, powers[:block_len], precision=PRECISE)
    decays = jnp.broadcast_to(powers[block_len], start_states.shape)
    _, totals = lax.associative_scan(chain_link, (decays[::-1], start_states[::-1]), axis=0)
    totals = totals[::-1]
    distance = block_len * jnp.arange(block_count, 0, -1, dtype=jnp.float32)
    states = totals + jnp.exp(-decay[None] * distance[:, None, None]) * carry_back[None]
    after = jnp.concatenate([states[1:], carry_back[None]], 0)
    return (after, totals[0])


def forward_work(lines, tables, block_len):
    decay, weight, carry_in = tables
    positions, powers, unit_scale, mode_coef, toeplitz, lag_table = prepare(
        decay, weight, block_len
    )
    in_blocks = lines[0].reshape(-1, block_len, lines[0].shape[1])
    before, _ = forward_states(in_blocks, powers, decay, carry_in, block_len)
    within_block = jnp.einsum("bsc,tsc->btc", in_blocks, toeplitz, precision=PRECISE)
    from_carry = jnp.einsum("bcn,tcn->btc", before, powers[1:] * mode_coef[None], precision=PRECISE)
    return (within_block + from_carry).reshape(lines[0].shape)


def backward_work(lines, tables, block_len):
    decay, weight, carry_in, carry_back = tables
    positions, powers, unit_scale, mode_coef, toeplitz, lag_table = prepare(
        decay, weight, block_len
    )
    in_blocks = lines[0].reshape(-1, block_len, lines[0].shape[1])
    back_blocks = lines[1].reshape(-1, block_len, lines[1].shape[1])
    before, _ = forward_states(in_blocks, powers, decay, carry_in, block_len)
    after, _ = backward_states(back_blocks, powers, decay, carry_back, block_len)
    within_block = jnp.einsum("btc,tsc->bsc", back_blocks, toeplitz, precision=PRECISE)
    from_carry = jnp.einsum(
        "bcn,scn->bsc", after, powers[1:][::-1] * mode_coef[None], precision=PRECISE
    )
    adjoint = (within_block + from_carry).reshape(lines[1].shape)
    carried = jnp.einsum("btc,tcn,bcn->cn", back_blocks, powers[1:], before, precision=PRECISE)
    pairs = jnp.einsum("btc,bsc->tsc", back_blocks, in_blocks, precision=PRECISE)
    pairs = jnp.where((lag_table >= 0)[:, :, None], pairs, 0.0)
    rising = jnp.exp(decay[None] * positions[:block_len, None, None])
    inside = jnp.einsum("tsc,tcn,scn->cn", pairs, powers[:block_len], rising, precision=PRECISE)
    return (adjoint, unit_scale * (carried + inside))


def to_groups(line_array, group_width):
    seq_rows, channels = line_array.shape
    return jnp.moveaxis(line_array.reshape(seq_rows, channels // group_width, group_width), 1, 0)


def from_groups(stacked):
    group_count, seq_rows, group_width = stacked.shape
    return jnp.moveaxis(stacked, 0, 1).reshape(seq_rows, group_count * group_width)


def param_groups(param_table, group_width):
    return param_table.reshape(
        param_table.shape[0] // group_width, group_width, param_table.shape[1]
    )


def grouped(work_fn, lines, tables, group_width):
    stacked_lines = tuple((to_groups(item, group_width) for item in lines))
    stacked_tables = tuple((param_groups(item, group_width) for item in tables))
    return lax.map(lambda packed: work_fn(packed[0], packed[1]), (stacked_lines, stacked_tables))


def flat_table(stacked):
    return stacked.reshape(stacked.shape[0] * stacked.shape[1], stacked.shape[2])


def shards(queries, keys_in, values_in, decay_rates, residues, skip_gain, cotangent):
    seq_rows, channels = queries.shape
    mode_count = decay_rates.shape[1]
    queries_f = queries.astype(jnp.float32)
    keys_f = keys_in.astype(jnp.float32)
    values_f = values_in.astype(jnp.float32)
    cot_f = cotangent.astype(jnp.float32)
    gated = lax.optimization_barrier((keys_f * values_f).astype(jnp.bfloat16))
    pulled = lax.optimization_barrier((cot_f * queries_f).astype(jnp.bfloat16))
    ctx_count = lax.axis_size("ctx")
    piece_width = channels // ctx_count
    offset = lax.axis_index("ctx") * piece_width
    own_rates = lax.dynamic_slice_in_dim(decay_rates, offset, piece_width, 0)
    own_residues = lax.dynamic_slice_in_dim(residues, offset, piece_width, 0)
    block_len = math.gcd(seq_rows * ctx_count, 128)
    group_width = math.gcd(piece_width, 64)
    zero_state = jnp.zeros((piece_width, mode_count), jnp.float32)
    line_in = lax.all_to_all(gated, "ctx", split_axis=1, concat_axis=0, tiled=True).astype(
        jnp.float32
    )
    conv_line = from_groups(
        grouped(
            partial(forward_work, block_len=block_len),
            (line_in,),
            (own_rates, own_residues, zero_state),
            group_width,
        )
    )
    convolved = lax.all_to_all(
        conv_line.astype(jnp.bfloat16), "ctx", split_axis=0, concat_axis=1, tiled=True
    )
    line_back = lax.all_to_all(pulled, "ctx", split_axis=1, concat_axis=0, tiled=True).astype(
        jnp.float32
    )
    adj_line, raw_grad = grouped(
        partial(backward_work, block_len=block_len),
        (line_in, line_back),
        (own_rates, own_residues, zero_state, zero_state),
        group_width,
    )
    adjoint = lax.all_to_all(
        from_groups(adj_line).astype(jnp.bfloat16), "ctx", split_axis=0, concat_axis=1, tiled=True
    )
    own_raw = flat_table(raw_grad)
    mixed = convolved.astype(jnp.float32) + skip_gain[None, :] * gated.astype(jnp.float32)
    operator_out = (queries_f * mixed).astype(jnp.bfloat16)
    grad_queries = (cot_f * mixed).astype(jnp.bfloat16)
    grad_gated = adjoint.astype(jnp.float32) + skip_gain[None, :] * pulled.astype(jnp.float32)
    grad_keys = (grad_gated * values_f).astype(jnp.bfloat16)
    grad_values = (grad_gated * keys_f).astype(jnp.bfloat16)
    raw_all = lax.all_gather(own_raw, "ctx", axis=0, tiled=True)
    grad_square = lax.psum(jnp.sum(raw_all * raw_all), "tp")
    factor = jnp.minimum(1.0, math.sqrt(D * ORDER) / jnp.sqrt(grad_square + 1e-06))
    grad_residues = raw_all * factor
    return (operator_out, grad_queries, grad_keys, grad_values, grad_residues)


def solution(mesh):
    in_specs = (
        P("ctx", "tp"),
        P("ctx", "tp"),
        P("ctx", "tp"),
        P("tp", None),
        P("tp", None),
        P("tp"),
        P("ctx", "tp"),
    )
    out_specs = (P("ctx", "tp"), P("ctx", "tp"), P("ctx", "tp"), P("ctx", "tp"), P("tp", None))
    return jax.shard_map(shards, mesh=mesh, in_specs=in_specs, out_specs=out_specs, check_vma=False)
```

profile of v0, /device:TPU:0, one launch (start us, length us, event | category | flops | bytes accessed | tf_op | source)
XLA Modules:
  0.0 889.6 jit_solution(15720263083457227983)
XLA Ops:
  13.1 13.2 %all-to-all-done = bf16[128,8,256]{2,0,1:T(8,128)(2,1)S(1)} async-done(((bf16[128,8,256]{2,0,1:T(8,128)(2,1)}), bf16[128,8,256]{2,0,1:T(8,128)(2,1)S(1)}, u32[]{:S(2)}, u32[]{:S(2)}) %all-to-all-start) | async-done | bytes 524320 | tf_op jit(solution)/shard_map/all_to_all | solution.py:131
  31.0 322.5 %while.22 = (s32[]{:T(128)}, bf16[4,1024,64]{1,2,0:T(8,128)(2,1)}, f32[4,64,16]{1,2,0:T(8,128)}, f32[4,64,16]{1,2,0:T(8,128)}, f32[4,1024,64]{1,2,0:T(8,128)}, /*index=5*/s32[]{:T(128)}, f32[]{:T(128)}) while((s32[]{:T(128)}, bf16[4,1024,64]{1,2,0:T(8,128)(2,1)}, f32[4,64,16]{1,2,0:T(8,128)}, f32[4,64,16]{1,2,0:T(8,128)}, ...), condition=%wide.region_1.2_spmd, body=%wide.region_0.1_spmd.sunk | while | flops 127683600 | bytes 32035488 | solution.py:107
  40.8 54.4 %gather_fusion = f32[16384,64]{1,0:T(8,128)} fusion(f32[128,64]{1,0:T(8,128)S(1)} %bitcast.246, s32[16384]{0:T(1024)S(1)} %bitcast_clamp_fusion.4), kind=kCustom, calls=%fused_computation.clone.1 | custom fusion | bytes 8454144 | tf_op jit(solution)/shard_map/while/body/eval_jaxpr/gather | solution.py:27
  102.6 8.3 fusion.142
  121.4 54.4 %gather_fusion = f32[16384,64]{1,0:T(8,128)} fusion(f32[128,64]{1,0:T(8,128)S(1)} %bitcast.246, s32[16384]{0:T(1024)S(1)} %bitcast_clamp_fusion.4), kind=kCustom, calls=%fused_computation.clone.1 | custom fusion | bytes 8454144 | tf_op jit(solution)/shard_map/while/body/eval_jaxpr/gather | solution.py:27
  202.0 54.4 %gather_fusion = f32[16384,64]{1,0:T(8,128)} fusion(f32[128,64]{1,0:T(8,128)S(1)} %bitcast.246, s32[16384]{0:T(1024)S(1)} %bitcast_clamp_fusion.4), kind=kCustom, calls=%fused_computation.clone.1 | custom fusion | bytes 8454144 | tf_op jit(solution)/shard_map/while/body/eval_jaxpr/gather | solution.py:27
  282.7 54.4 %gather_fusion = f32[16384,64]{1,0:T(8,128)} fusion(f32[128,64]{1,0:T(8,128)S(1)} %bitcast.246, s32[16384]{0:T(1024)S(1)} %bitcast_clamp_fusion.4), kind=kCustom, calls=%fused_computation.clone.1 | custom fusion | bytes 8454144 | tf_op jit(solution)/shard_map/while/body/eval_jaxpr/gather | solution.py:27
  361.0 13.7 %all-to-all-done.1 = bf16[8,128,256]{2,1,0:T(8,128)(2,1)S(1)} async-done(((bf16[8,128,256]{2,1,0:T(8,128)(2,1)}), bf16[8,128,256]{2,1,0:T(8,128)(2,1)S(1)}, u32[]{:S(2)}, u32[]{:S(2)}) %all-to-all-start.1) | async-done | bytes 524320 | tf_op jit(solution)/shard_map/all_to_all | solution.py:142
  380.9 15.3 %all-to-all-done.2 = bf16[128,8,256]{2,0,1:T(8,128)(2,1)S(1)} async-done(((bf16[128,8,256]{2,0,1:T(8,128)(2,1)}), bf16[128,8,256]{2,0,1:T(8,128)(2,1)S(1)}, u32[]{:S(2)}, u32[]{:S(2)}) %all-to-all-start.2) | async-done | bytes 524320 | tf_op jit(solution)/shard_map/all_to_all | solution.py:145
  398.7 447.0 %while.23 = (s32[]{:T(128)}, bf16[4,1024,64]{1,2,0:T(8,128)(2,1)}, f32[4,64,16]{2,1,0:T(8,128)}, f32[4,64,16]{1,2,0:T(8,128)}, f32[4,64,16]{1,2,0:T(8,128)}, /*i...) while((s32[]{:T(128)}, bf16[4,1024,64]{1,2,0:T(8,128)(2,1)}, ...), condition=%wide.region_3.4_spmd, body=%wide.region_2.3_spmd.sunk | while | flops 457695264 | bytes 48635332 | solution.py:107
  426.8 8.5 fusion.173
  438.2 54.4 %gather_fusion.1 = f32[16384,64]{1,0:T(8,128)} fusion(f32[128,64]{1,0:T(8,128)S(1)} %bitcast.247, s32[16384]{0:T(1024)S(1)} %bitcast_clamp_fusion.5), kind=kCustom, calls=%fused_computation.1.clone.1 | custom fusion | bytes 8454144 | tf_op jit(solution)/shard_map/while/body/eval_jaxpr/gather | solution.py:27
  492.6 8.8 copy.328
  538.6 8.5 fusion.173
  549.9 54.4 %gather_fusion.1 = f32[16384,64]{1,0:T(8,128)} fusion(f32[128,64]{1,0:T(8,128)S(1)} %bitcast.247, s32[16384]{0:T(1024)S(1)} %bitcast_clamp_fusion.5), kind=kCustom, calls=%fused_computation.1.clone.1 | custom fusion | bytes 8454144 | tf_op jit(solution)/shard_map/while/body/eval_jaxpr/gather | solution.py:27
  604.3 8.8 copy.328
  650.3 8.5 fusion.173
  661.7 54.4 %gather_fusion.1 = f32[16384,64]{1,0:T(8,128)} fusion(f32[128,64]{1,0:T(8,128)S(1)} %bitcast.247, s32[16384]{0:T(1024)S(1)} %bitcast_clamp_fusion.5), kind=kCustom, calls=%fused_computation.1.clone.1 | custom fusion | bytes 8454144 | tf_op jit(solution)/shard_map/while/body/eval_jaxpr/gather | solution.py:27
  716.1 8.8 copy.328
  762.1 8.5 fusion.173
  773.4 54.4 %gather_fusion.1 = f32[16384,64]{1,0:T(8,128)} fusion(f32[128,64]{1,0:T(8,128)S(1)} %bitcast.247, s32[16384]{0:T(1024)S(1)} %bitcast_clamp_fusion.5), kind=kCustom, calls=%fused_computation.1.clone.1 | custom fusion | bytes 8454144 | tf_op jit(solution)/shard_map/while/body/eval_jaxpr/gather | solution.py:27
  827.8 8.8 copy.328
  853.8 19.5 %all_gather.3 = f32[2048,16]{0,1:T(8,128)S(1)} all-gather(f32[256,16]{0,1:T(8,128)S(1)} %copy.282), channel_id=1, replica_groups=mesh['ctx'=8,'tp'=4] {'ctx'}, dimensions={0}, use_global_device_ids=true | all-gather | bytes 147456 | tf_op jit(solution)/shard_map/all_gather | solution.py:164
  874.9 10.5 %psum.7 = f32[]{:T(128)} all-reduce(f32[]{:T(128)} %multiply_reduce_fusion.1), channel_id=1, replica_groups=mesh['ctx'=8,'tp'=4] {'tp'}, use_global_device_ids=true, to_apply=%region_5.6 | all-reduce | flops 1 | bytes 8 | tf_op jit(solution)/shard_map/psum | solution.py:165
  (558 shorter events, 300.6 us)
Async XLA Ops:
  1.9 25.8 %copy-start.2 = (bf16[128,2048]{0,1:T(8,128)(2,1)}, bf16[128,2048]{0,1:T(8,128)(2,1)S(1)}, u32[]{:S(2)}) copy-start(bf16[128,2048]{0,1:T(8,128)(2,1)S(1)} %copy.241) | copy-start | bytes 1572868
  3.5 26.7 %copy-start.4 = (bf16[128,2048]{0,1:T(8,128)(2,1)}, bf16[128,2048]{0,1:T(8,128)(2,1)S(1)}, u32[]{:S(2)}) copy-start(bf16[128,2048]{0,1:T(8,128)(2,1)S(1)} %copy.242) | copy-start | bytes 1572868
  3.6 27.4 %copy-start = (bf16[128,2048]{0,1:T(8,128)(2,1)}, bf16[128,2048]{0,1:T(8,128)(2,1)S(1)}, u32[]{:S(2)}) copy-start(bf16[128,2048]{0,1:T(8,128)(2,1)S(1)} %fusion.53) | copy-start | bytes 1572868
  4.6 21.7 %all-to-all-start = ((bf16[128,8,256]{2,0,1:T(8,128)(2,1)}), bf16[128,8,256]{2,0,1:T(8,128)(2,1)S(1)}, u32[]{:S(2)}, u32[]{:S(2)}) async-start(bf16[128,8,256]{2,0,1:T(8,128)(2,1)} %copy.243), calls=%async_computation | async-start | bytes 1048576 | tf_op jit(solution)/shard_map/all_to_all | solution.py:131
  353.5 21.4 %copy-start.1 = (bf16[128,2048]{0,1:T(8,128)(2,1)S(1)}, bf16[128,2048]{0,1:T(8,128)(2,1)}, u32[]{:S(2)}) copy-start(bf16[128,2048]{0,1:T(8,128)(2,1)} %copy-done) | copy-start | bytes 1572868
  353.5 21.4 %copy-start.16 = (f32[2048]{0:T(1024)S(1)}, f32[2048]{0:T(1024)}, u32[]{:S(2)}) copy-start(f32[2048]{0:T(1024)} %param.16) | copy-start | bytes 24580
  355.9 18.8 %all-to-all-start.1 = ((bf16[8,128,256]{2,1,0:T(8,128)(2,1)}), bf16[8,128,256]{2,1,0:T(8,128)(2,1)S(1)}, u32[]{:S(2)}, u32[]{:S(2)}) async-start(bf16[8,128,256]{2,1,0:T(8,128)(2,1)} %copy.247), calls=%async_computation.1 | async-start | bytes 1048576 | tf_op jit(solution)/shard_map/all_to_all | solution.py:142
  376.4 22.3 %copy-start.6 = (bf16[128,2048]{0,1:T(8,128)(2,1)}, bf16[128,2048]{0,1:T(8,128)(2,1)S(1)}, u32[]{:S(2)}) copy-start(bf16[128,2048]{0,1:T(8,128)(2,1)S(1)} %get-tuple-element.165) | copy-start | bytes 1572868
  377.4 18.8 %all-to-all-start.2 = ((bf16[128,8,256]{2,0,1:T(8,128)(2,1)}), bf16[128,8,256]{2,0,1:T(8,128)(2,1)S(1)}, u32[]{:S(2)}, u32[]{:S(2)}) async-start(bf16[128,8,256]{2,0,1:T(8,128)(2,1)} %copy.250), calls=%async_computation.2 | async-start | bytes 1048576 | tf_op jit(solution)/shard_map/all_to_all | solution.py:145
  415.6 11.0 %copy-start.11 = (f32[1,64,16]{1,2,0:T(8,128)S(1)}, f32[1,64,16]{1,2,0:T(8,128)}, u32[]{:S(2)}) copy-start(f32[1,64,16]{1,2,0:T(8,128)} %copy-done.10) | copy-start | bytes 12292 | tf_op jit(solution)/shard_map/while
  418.5 17.6 %copy-start.12 = (f32[64,16]{0,1:T(8,128)S(1)}, f32[64,16]{0,1:T(8,128)}, u32[]{:S(2)}) copy-start(f32[64,16]{0,1:T(8,128)} %get-tuple-element.284) | copy-start | bytes 12292 | tf_op jit(solution)/shard_map/while
  527.4 11.0 %copy-start.11 = (f32[1,64,16]{1,2,0:T(8,128)S(1)}, f32[1,64,16]{1,2,0:T(8,128)}, u32[]{:S(2)}) copy-start(f32[1,64,16]{1,2,0:T(8,128)} %copy-done.10) | copy-start | bytes 12292 | tf_op jit(solution)/shard_map/while
  530.2 17.6 %copy-start.12 = (f32[64,16]{0,1:T(8,128)S(1)}, f32[64,16]{0,1:T(8,128)}, u32[]{:S(2)}) copy-start(f32[64,16]{0,1:T(8,128)} %get-tuple-element.284) | copy-start | bytes 12292 | tf_op jit(solution)/shard_map/while
  639.2 11.0 %copy-start.11 = (f32[1,64,16]{1,2,0:T(8,128)S(1)}, f32[1,64,16]{1,2,0:T(8,128)}, u32[]{:S(2)}) copy-start(f32[1,64,16]{1,2,0:T(8,128)} %copy-done.10) | copy-start | bytes 12292 | tf_op jit(solution)/shard_map/while
  642.0 17.6 %copy-start.12 = (f32[64,16]{0,1:T(8,128)S(1)}, f32[64,16]{0,1:T(8,128)}, u32[]{:S(2)}) copy-start(f32[64,16]{0,1:T(8,128)} %get-tuple-element.284) | copy-start | bytes 12292 | tf_op jit(solution)/shard_map/while
  750.9 11.0 %copy-start.11 = (f32[1,64,16]{1,2,0:T(8,128)S(1)}, f32[1,64,16]{1,2,0:T(8,128)}, u32[]{:S(2)}) copy-start(f32[1,64,16]{1,2,0:T(8,128)} %copy-done.10) | copy-start | bytes 12292 | tf_op jit(solution)/shard_map/while
  753.7 17.6 %copy-start.12 = (f32[64,16]{0,1:T(8,128)S(1)}, f32[64,16]{0,1:T(8,128)}, u32[]{:S(2)}) copy-start(f32[64,16]{0,1:T(8,128)} %get-tuple-element.284) | copy-start | bytes 12292 | tf_op jit(solution)/shard_map/while
  762.1 10.6 %copy-start.13 = (f32[1,64,16]{1,2,0:T(8,128)S(1)}, f32[1,64,16]{1,2,0:T(8,128)}, u32[]{:S(2)}) copy-start(f32[1,64,16]{1,2,0:T(8,128)} %get-tuple-element.304) | copy-start | bytes 12292 | tf_op jit(solution)/shard_map/while
  845.7 28.2 %copy-start.8 = (bf16[128,2048]{0,1:T(8,128)(2,1)S(1)}, bf16[128,2048]{0,1:T(8,128)(2,1)}, u32[]{:S(2)}) copy-start(bf16[128,2048]{0,1:T(8,128)(2,1)} %get-tuple-element.163) | copy-start | bytes 1572868
  845.7 41.4 %copy-start.3 = (bf16[128,2048]{0,1:T(8,128)(2,1)S(1)}, bf16[128,2048]{0,1:T(8,128)(2,1)}, u32[]{:S(2)}) copy-start(bf16[128,2048]{0,1:T(8,128)(2,1)} %copy-done.2) | copy-start | bytes 1572868
  845.7 41.4 %copy-start.5 = (bf16[128,2048]{0,1:T(8,128)(2,1)S(1)}, bf16[128,2048]{0,1:T(8,128)(2,1)}, u32[]{:S(2)}) copy-start(bf16[128,2048]{0,1:T(8,128)(2,1)} %copy-done.4) | copy-start | bytes 1572868
  845.7 41.4 %copy-start.7 = (bf16[128,2048]{0,1:T(8,128)(2,1)S(1)}, bf16[128,2048]{0,1:T(8,128)(2,1)}, u32[]{:S(2)}) copy-start(bf16[128,2048]{0,1:T(8,128)(2,1)} %copy-done.6) | copy-start | bytes 1572868
  845.7 41.4 %copy-start.17 = (f32[2048]{0:T(1024)S(1)}, f32[2048]{0:T(1024)}, u32[]{:S(2)}) copy-start(f32[2048]{0:T(1024)} %param.16) | copy-start | bytes 24580
  848.2 38.6 %all-to-all-start.3 = ((bf16[8,128,256]{2,1,0:T(8,128)(2,1)}), bf16[8,128,256]{2,1,0:T(8,128)(2,1)S(1)}, u32[]{:S(2)}, u32[]{:S(2)}) async-start(bf16[8,128,256]{2,1,0:T(8,128)(2,1)} %copy.254), calls=%async_computation.3 | async-start | bytes 1048576 | tf_op jit(solution)/shard_map/all_to_all | solution.py:154
  (13 other events, 51.6 us)
where the time goes:
time: 892 us; the launch traced here: 890 us
  local copies, waits for them, and re-layouts  603 us (68%)
  matrix products  167 us (19%)
  waiting for transfers between devices  42.2 us (5%)
  blocking collectives  30 us (3%)
  other arithmetic  26.9 us (3%)
  starting transfers between devices  16.8 us (2%)
    gather x16, local copies, waits for them, and re-layouts, prepare(): short_filter[jnp.maximum(lag_table, 0)]  500 us
    dot_general x4, matrix products, backward_work(): jnp.einsum('tsc,tcn,scn->cn', pairs, powers[:block_len], rising, precisio...  33.9 us
    dot_general x4, matrix products, forward_work(): jnp.einsum('bsc,tsc->btc', in_blocks, toeplitz, precision=PRECISE)  33.2 us
    dot_general x4, matrix products, backward_work(): jnp.einsum('btc,tsc->bsc', back_blocks, toeplitz, precision=PRECISE)  33.2 us
    dot_general x4, matrix products, backward_work(): jnp.einsum('btc,bsc->tsc', back_blocks, in_blocks, precision=PRECISE)  32.8 us
    while x84, local copies, waits for them, and re-layouts  29.4 us
    rev x16, local copies, waits for them, and re-layouts, forward_states(): powers[:block_len][::-1]  24.7 us
    all_gather x1, blocking collectives, shards(): raw_all = lax.all_gather(own_raw, 'ctx', axis=0, tiled=True)  19.5 us
  transfers between devices with their start and end apart: 4, of which 3 were waited for; matrix products, arithmetic and copies ran while one was open for 1% of the time, Pallas kernels for 0%

commit v1 on v0

v1 whole, which is shorter than its diff:
```python
import math

import jax
import jax.numpy as jnp
from jax import lax
from jax.experimental import pallas as pl
from jax.experimental.pallas import tpu as pltpu
from jax.sharding import PartitionSpec as P

F32 = jnp.float32
WIRE = jnp.bfloat16
LANES = 128
UNROLL = 8
VMEM_LIMIT = 40 * 1024 * 1024


def gate(left_ref, right_ref, cols):
    product = left_ref[:, cols].astype(F32) * right_ref[:, cols].astype(F32)
    return product.astype(jnp.bfloat16).astype(F32)


def rows_of(ref, step, sub, pitch):
    return ref[pl.ds(step, sub, stride=pitch), :]


def spread(table_ref, modes, sub, scratch):
    for s in range(sub):
        scratch[pl.ds(s, modes, stride=sub), :] = table_ref[:, s * LANES : (s + 1) * LANES]
    return [scratch[n * sub : (n + 1) * sub, :] for n in range(modes)]


def tree_sum(items):
    items = list(items)
    while len(items) > 1:
        items = [
            items[i] + items[i + 1] if i + 1 < len(items) else items[i]
            for i in range(0, len(items), 2)
        ]
    return items[0]


def fill_lines(k_ref, v_ref, q_ref, ct_ref, gated, pulled, sub, seq):
    for s in range(sub):
        cols = slice(s * LANES, (s + 1) * LANES)
        gated[s * seq : (s + 1) * seq, :] = gate(k_ref, v_ref, cols)
        pulled[s * seq : (s + 1) * seq, :] = gate(ct_ref, q_ref, cols)


def states_kernel(q_ref, k_ref, v_ref, ct_ref, rate_ref, out_ref, gated, pulled, table, states):
    seq = q_ref.shape[0]
    modes = rate_ref.shape[0]
    sub = q_ref.shape[1] // LANES
    fill_lines(k_ref, v_ref, q_ref, ct_ref, gated, pulled, sub, seq)
    decay = [jnp.exp(-r) for r in spread(rate_ref, modes, sub, table)]
    zeros = tuple(jnp.zeros((sub, LANES), F32) for _ in range(modes))

    def forward(i, carry):
        held, inner = list(carry[0]), list(carry[1])
        for u in range(UNROLL):
            t = i * UNROLL + u
            x = rows_of(gated, t, sub, seq)
            p = rows_of(pulled, t, sub, seq)
            for n in range(modes):
                held[n] = decay[n] * held[n] + x
                inner[n] = inner[n] + p * held[n]
        return tuple(held), tuple(inner)

    def backward(i, carry):
        held = list(carry)
        for u in range(UNROLL):
            t = seq - 1 - (i * UNROLL + u)
            p = rows_of(pulled, t, sub, seq)
            for n in range(modes):
                held[n] = decay[n] * held[n] + p
        return tuple(held)

    ends, inner = lax.fori_loop(0, seq // UNROLL, forward, (zeros, zeros))
    starts = lax.fori_loop(0, seq // UNROLL, backward, zeros)
    for n in range(modes):
        rows = slice(n * sub, (n + 1) * sub)
        states[0, rows, :] = ends[n]
        states[1, rows, :] = starts[n]
        states[2, rows, :] = inner[n]
    dests, _, slab, _ = out_ref.shape
    for d in range(dests):
        for kind in range(3):
            out_ref[d, kind] = states[kind, d * slab : (d + 1) * slab, :].astype(out_ref.dtype)


def local_kernel(
    q_ref, k_ref, v_ref, ct_ref, rate_ref, res_ref, conv_ref, adj_ref, gated, pulled, table
):
    seq = q_ref.shape[0]
    modes = rate_ref.shape[0]
    sub = q_ref.shape[1] // LANES
    fill_lines(k_ref, v_ref, q_ref, ct_ref, gated, pulled, sub, seq)
    rates = spread(rate_ref, modes, sub, table)
    weights = spread(res_ref, modes, sub, table)
    decay = [jnp.exp(-r) for r in rates]
    coef = [w * jnp.sqrt(1.0 - jnp.exp(-2.0 * r)) for w, r in zip(weights, rates)]
    zeros = tuple(jnp.zeros((sub, LANES), F32) for _ in range(modes))

    def scan(source, target, reverse):
        def body(i, carry):
            held = list(carry)
            for u in range(UNROLL):
                t = i * UNROLL + u
                if reverse:
                    t = seq - 1 - t
                x = rows_of(source, t, sub, seq)
                total = [None] * 4
                for n in range(modes):
                    held[n] = decay[n] * held[n] + x
                    term = coef[n] * held[n]
                    total[n % 4] = term if total[n % 4] is None else total[n % 4] + term
                target[0, t] = tree_sum(total)
            return tuple(held)

        lax.fori_loop(0, seq // UNROLL, body, zeros)

    scan(gated, conv_ref, False)
    scan(pulled, adj_ref, True)


def chunks_kernel(in_ref, rate_ref, out_ref):
    count = in_ref.shape[0]
    rate = rate_ref[...]
    step = jnp.exp(-rate)
    span = jnp.exp(-rate * CHUNK[0])
    unit = jnp.sqrt(1.0 - jnp.exp(-2.0 * rate))
    held = jnp.zeros_like(rate)
    total = jnp.zeros_like(rate)
    for j in range(count):
        out_ref[j, 0] = held.astype(out_ref.dtype)
        start = in_ref[j, 1].astype(F32)
        total = total + (in_ref[j, 2].astype(F32) + step * start * held)
        held = span * held + in_ref[j, 0].astype(F32)
    back = jnp.zeros_like(rate)
    raw = (unit * total).astype(out_ref.dtype)
    for j in reversed(range(count)):
        out_ref[j, 1] = back.astype(out_ref.dtype)
        out_ref[j, 2] = raw
        back = span * back + in_ref[j, 1].astype(F32)


CHUNK = [128]


def finish_kernel(
    q_ref,
    k_ref,
    v_ref,
    ct_ref,
    rate_ref,
    res_ref,
    skip_ref,
    conv_ref,
    adj_ref,
    in_ref,
    out_ref,
    gq_ref,
    gk_ref,
    gv_ref,
    raw_ref,
    conv_lines,
    adj_lines,
    table,
    states,
):
    seq = q_ref.shape[0]
    modes = rate_ref.shape[0]
    sub = q_ref.shape[1] // LANES
    sources, _, slab, _ = in_ref.shape
    for d in range(sources):
        for kind in range(3):
            states[kind, d * slab : (d + 1) * slab, :] = in_ref[d, kind].astype(F32)
    for s in range(sub):
        raw_ref[:, s * LANES : (s + 1) * LANES] = states[2, pl.ds(s, modes, stride=sub), :]
    rates = spread(rate_ref, modes, sub, table)
    weights = spread(res_ref, modes, sub, table)
    decay = [jnp.exp(-r) for r in rates]
    coef = [w * jnp.sqrt(1.0 - jnp.exp(-2.0 * r)) for w, r in zip(weights, rates)]
    ahead = tuple(coef[n] * states[0, n * sub : (n + 1) * sub, :] for n in range(modes))
    behind = tuple(coef[n] * states[1, n * sub : (n + 1) * sub, :] for n in range(modes))

    def body(i, carry):
        ahead, behind = list(carry[0]), list(carry[1])
        for u in range(UNROLL):
            t = i * UNROLL + u
            back_t = seq - 1 - t
            total_a, total_b = [None] * 4, [None] * 4
            for n in range(modes):
                ahead[n] = decay[n] * ahead[n]
                behind[n] = decay[n] * behind[n]
                total_a[n % 4] = ahead[n] if n < 4 else total_a[n % 4] + ahead[n]
                total_b[n % 4] = behind[n] if n < 4 else total_b[n % 4] + behind[n]
            conv_lines[pl.ds(t, sub, stride=seq), :] = conv_ref[0, t] + tree_sum(total_a)
            adj_lines[pl.ds(back_t, sub, stride=seq), :] = adj_ref[0, back_t] + tree_sum(total_b)
        return tuple(ahead), tuple(behind)

    lax.fori_loop(0, seq // UNROLL, body, (ahead, behind))
    for s in range(sub):
        cols = slice(s * LANES, (s + 1) * LANES)
        rows = slice(s * seq, (s + 1) * seq)
        skip = skip_ref[:, cols]
        q, ct = q_ref[:, cols].astype(F32), ct_ref[:, cols].astype(F32)
        k, v = k_ref[:, cols].astype(F32), v_ref[:, cols].astype(F32)
        gated = (k * v).astype(jnp.bfloat16).astype(F32)
        pulled = (ct * q).astype(jnp.bfloat16).astype(F32)
        mixed = conv_lines[rows, :].astype(jnp.bfloat16).astype(F32) + skip * gated
        out_ref[:, cols] = (q * mixed).astype(out_ref.dtype)
        gq_ref[:, cols] = (ct * mixed).astype(gq_ref.dtype)
        grad = adj_lines[rows, :].astype(jnp.bfloat16).astype(F32) + skip * pulled
        gk_ref[:, cols] = (grad * v).astype(gk_ref.dtype)
        gv_ref[:, cols] = (grad * k).astype(gv_ref.dtype)


def shards(queries, keys_in, values_in, decay_rates, residues, skip_gain, cotangent):
    seq, channels = queries.shape
    modes = decay_rates.shape[1]
    ctx = lax.axis_size("ctx")
    tp = lax.axis_size("tp")
    groups = channels // LANES
    sub = math.gcd(groups, 8)
    blocks = groups // sub
    width = sub * LANES
    slab = modes * groups // ctx
    per_block = ctx // blocks
    block_rows = modes * sub
    rates, weights = decay_rates.T, residues.T
    params = pltpu.CompilerParams(vmem_limit_bytes=VMEM_LIMIT)

    line_spec = pl.BlockSpec((seq, width), lambda b: (0, b))
    table_spec = pl.BlockSpec((modes, width), lambda b: (0, b))
    pack_spec = pl.BlockSpec((per_block, 3, slab, LANES), lambda b: (b, 0, 0, 0))
    tall_spec = pl.BlockSpec((1, seq, sub, LANES), lambda b: (b, 0, 0, 0))
    lines_scratch = pltpu.VMEM((sub * seq, LANES), F32)
    table_scratch = pltpu.VMEM((block_rows, LANES), F32)
    states_scratch = pltpu.VMEM((3, block_rows, LANES), F32)
    elements = seq * channels * modes

    packed = pl.pallas_call(
        states_kernel,
        grid=(blocks,),
        in_specs=[line_spec] * 4 + [table_spec],
        out_specs=pack_spec,
        out_shape=jax.ShapeDtypeStruct((ctx, 3, slab, LANES), WIRE),
        scratch_shapes=[lines_scratch, lines_scratch, table_scratch, states_scratch],
        compiler_params=params,
        cost_estimate=pl.CostEstimate(
            flops=6 * elements, bytes_accessed=8 * seq * channels, transcendentals=0
        ),
        name="chunk_states",
    )(queries, keys_in, values_in, cotangent, rates)
    gathered = lax.all_to_all(packed, "ctx", split_axis=0, concat_axis=0, tiled=True)

    conv, adj = pl.pallas_call(
        local_kernel,
        grid=(blocks,),
        in_specs=[line_spec] * 4 + [table_spec] * 2,
        out_specs=[tall_spec] * 2,
        out_shape=[jax.ShapeDtypeStruct((blocks, seq, sub, LANES), F32)] * 2,
        scratch_shapes=[lines_scratch, lines_scratch, table_scratch],
        compiler_params=params,
        cost_estimate=pl.CostEstimate(
            flops=8 * elements, bytes_accessed=16 * seq * channels, transcendentals=0
        ),
        name="local_conv",
    )(queries, keys_in, values_in, cotangent, rates, weights)

    own_rates = lax.dynamic_slice_in_dim(
        rates.reshape(modes, blocks, sub, LANES).transpose(1, 0, 2, 3).reshape(-1, LANES),
        lax.axis_index("ctx") * slab,
        slab,
        0,
    )
    CHUNK[0] = seq
    carries = pl.pallas_call(
        chunks_kernel,
        out_shape=jax.ShapeDtypeStruct((ctx, 3, slab, LANES), WIRE),
        name="chunk_scan",
    )(gathered, own_rates)
    carried = lax.all_to_all(carries, "ctx", split_axis=0, concat_axis=0, tiled=True)

    raw_rows = carried[:, 2].astype(F32)
    square = jnp.sum(raw_rows * raw_rows)
    if tp <= 4:
        shares = [
            lax.ppermute(square, "tp", [(i, (i + hop) % tp) for i in range(tp)])
            for hop in range(1, tp)
        ]
    else:
        shares = None

    operator_out, grad_queries, grad_keys, grad_values, raw = pl.pallas_call(
        finish_kernel,
        grid=(blocks,),
        in_specs=[line_spec] * 4
        + [table_spec] * 2
        + [pl.BlockSpec((1, width), lambda b: (0, b))]
        + [tall_spec] * 2
        + [pack_spec],
        out_specs=[line_spec] * 4 + [table_spec],
        out_shape=[jax.ShapeDtypeStruct((seq, channels), jnp.bfloat16)] * 4
        + [jax.ShapeDtypeStruct((modes, channels), F32)],
        scratch_shapes=[lines_scratch, lines_scratch, table_scratch, states_scratch],
        compiler_params=params,
        cost_estimate=pl.CostEstimate(
            flops=4 * elements, bytes_accessed=24 * seq * channels, transcendentals=0
        ),
        name="finish",
    )(
        queries,
        keys_in,
        values_in,
        cotangent,
        rates,
        weights,
        skip_gain.reshape(1, channels),
        conv,
        adj,
        carried,
    )
    if shares is None:
        grad_square = lax.psum(square, "tp")
    else:
        grad_square = square
        for share in shares:
            grad_square = grad_square + share
    limit = math.sqrt(channels * tp * modes)
    factor = jnp.minimum(1.0, limit / jnp.sqrt(grad_square + 1e-06))
    return (operator_out, grad_queries, grad_keys, grad_values, (raw * factor).T)


def solution(mesh):
    lines, tables = P("ctx", "tp"), P("tp", None)
    in_specs = (lines, lines, lines, tables, tables, P("tp"), lines)
    out_specs = (lines, lines, lines, lines, tables)
    return jax.shard_map(shards, mesh=mesh, in_specs=in_specs, out_specs=out_specs, check_vma=False)
```

time: 892 us -> 58.9 us (0.07)
  local copies, waits for them, and re-layouts: 603 us -> 11.1 us
  matrix products: 167 us -> 0 us
  waiting for transfers between devices: 42.2 us -> 7.65 us
  blocking collectives: 30 us -> 0 us
  other arithmetic: 26.9 us -> 2.22 us
  Pallas kernels: 0 us -> 19.6 us
    gather x16 -> x0, local copies, waits for them, and re-layouts: 500 us -> none  [prepare(): short_filter[jnp.maximum(lag_table, 0)]]
    dot_general x44 -> x0, matrix products: 167 us -> none  [the longest x4 33.9 us: backward_work(): jnp.einsum('tsc,tcn,scn->cn', pairs, powers[:block_len], rising, precisio...]
    all_to_all x4 -> x2, waiting for transfers between devices: 42.2 us -> 7.64 us  [the longest x1 7.64 us: shards(): lax.all_to_all(packed, 'ctx', split_axis=0, concat_axis=0, tiled=True)]
    while x86 -> x0, local copies, waits for them, and re-layouts: 30.6 us -> none
    rev x20 -> x0, local copies, waits for them, and re-layouts: 24.7 us -> none  [the longest x16 24.7 us: forward_states(): powers[:block_len][::-1]]
    pallas_call x0 -> x4, Pallas kernels: none -> 19.6 us  [the longest x1 6.48 us: shards(): pl.pallas_call(states_kernel, grid=(blocks,), in_specs=[line_spec] * 4 +...]
    all_gather x1 -> x0, blocking collectives: 19.5 us -> none  [shards(): raw_all = lax.all_gather(own_raw, 'ctx', axis=0, tiled=True)]
    psum x1 -> x0, blocking collectives: 10.5 us -> none  [shards(): grad_square = lax.psum(jnp.sum(raw_all * raw_all), 'tp')]
  transfers between devices with their start and end apart: 4 -> 5, of which waited for: 3 -> 1; matrix products, arithmetic and copies ran while one was open for 1% -> 1% of each run, Pallas kernels for 0% -> 20%
where the time goes in v1:
time: 58.9 us; the launch traced here: 58.2 us
  Pallas kernels  19.6 us (33%)
  starting transfers between devices  14.3 us (24%)
  local copies, waits for them, and re-layouts  11.1 us (19%)
  waiting for transfers between devices  7.65 us (13%)
  between operations  3.33 us (6%)
  other arithmetic  2.22 us (4%)
    unnamed x35, local copies, waits for them, and re-layouts  10.5 us
    all_to_all x1, waiting for transfers between devices, shards(): lax.all_to_all(packed, 'ctx', split_axis=0, concat_axis=0, tiled=True)  7.64 us
    pallas_call x1, Pallas kernels, shards(): pl.pallas_call(states_kernel, grid=(blocks,), in_specs=[line_spec] * 4 +...  6.48 us
    all_to_all x1, starting transfers between devices, shards(): lax.all_to_all(packed, 'ctx', split_axis=0, concat_axis=0, tiled=True)  6.46 us
    pallas_call x1, Pallas kernels, shards(): pl.pallas_call(local_kernel, grid=(blocks,), in_specs=[line_spec] * 4 + [...  6.32 us
    pallas_call x1, Pallas kernels, shards(): pl.pallas_call(finish_kernel, grid=(blocks,), in_specs=[line_spec] * 4 +...  5.13 us
    ppermute x3, starting transfers between devices, shards(): lax.ppermute(square, 'tp', [(i, (i + hop) % tp) for i in range(tp)])  4.47 us
    all_to_all x1, starting transfers between devices, shards(): lax.all_to_all(carries, 'ctx', split_axis=0, concat_axis=0, tiled=True)  3.39 us
  transfers between devices with their start and end apart: 5, of which 1 were waited for; matrix products, arithmetic and copies ran while one was open for 1% of the time, Pallas kernels for 20%

profile of v1, /device:TPU:0, one launch (start us, length us, event | category | flops | bytes accessed | tf_op | source)
XLA Modules:
  0.0 58.2 jit_solution(14853230102522462619)
XLA Ops:
  0.6 1.0 %copy-done = bf16[128,2048]{1,0:T(8,128)(2,1)S(1)} copy-done((bf16[128,2048]{1,0:T(8,128)(2,1)S(1)}, bf16[128,2048]{1,0:T(8,128)(2,1)}, u32[]{:S(2)}) %copy-start) | copy-done | bytes 524312
  1.7 1.0 %copy-done.2 = bf16[128,2048]{1,0:T(8,128)(2,1)S(1)} copy-done((bf16[128,2048]{1,0:T(8,128)(2,1)S(1)}, bf16[128,2048]{1,0:T(8,128)(2,1)}, u32[]{:S(2)}) %copy-start.2) | copy-done | bytes 524312
  2.7 1.0 %copy-done.4 = bf16[128,2048]{1,0:T(8,128)(2,1)S(1)} copy-done((bf16[128,2048]{1,0:T(8,128)(2,1)S(1)}, bf16[128,2048]{1,0:T(8,128)(2,1)}, u32[]{:S(2)}) %copy-start.4) | copy-done | bytes 524312
  3.8 1.0 %copy-done.6 = bf16[128,2048]{1,0:T(8,128)(2,1)S(1)} copy-done((bf16[128,2048]{1,0:T(8,128)(2,1)S(1)}, bf16[128,2048]{1,0:T(8,128)(2,1)}, u32[]{:S(2)}) %copy-start.6) | copy-done | bytes 524312
  4.8 0.9 %copy-done.8 = f32[2048,16]{0,1:T(8,128)S(1)} copy-done((f32[2048,16]{0,1:T(8,128)S(1)}, f32[2048,16]{0,1:T(8,128)}, u32[]{:S(2)}) %copy-start.8) | copy-done | bytes 131096
  5.7 6.5 %chunk_states.1 = bf16[8,3,32,128]{3,2,1,0:T(8,128)(2,1)} custom-call(bf16[128,2048]{1,0:T(8,128)(2,1)S(1)} %copy-done, bf16[128,2048]{1,0:T(8,128)(2,1)S(1)} %copy-done.2, bf16[128,2048]{1,0:T(8,128)(2,1)S(1)} %copy-done.4, bf16[128,2048]{1,0:T(8,128)(2,1)S(1)} %copy-done.6, f32[16,2048]{1,0:T(8,128)S(1)} %bitcast.11), custom_call_target="tpu_custom_call" | custom-call | flops 25165824 | bytes 2097152 | tf_op jit(solution)/shard_map/chunk_states/pallas_call | solution.py:242
  12.2 6.5 %all-to-all-start = ((bf16[8,3,32,128]{3,2,1,0:T(8,128)(2,1)}), bf16[8,3,32,128]{3,2,1,0:T(8,128)(2,1)S(1)}, u32[]{:S(2)}, u32[]{:S(2)}) async-start(bf16[8,3,32,128]{3,2,1,0:T(8,128)(2,1)} %chunk_states.1), calls=%async_computation | async-start | bytes 393216 | tf_op jit(solution)/shard_map/all_to_all | solution.py:255
  18.7 0.6 %constant_dynamic-slice_fusion.rate_ref = f32[32,128]{1,0:T(8,128)} fusion(f32[256,128]{1,0:T(8,128)S(1)} %bitcast.19, s32[]{:T(128)S(6)} %select_n.3), kind=kLoop, calls=%fused_computation.2 | loop fusion | bytes 32772 | tf_op jit(solution)/shard_map/dynamic_slice | solution.py:271
  19.4 7.6 %all-to-all-done.in_ref = bf16[8,3,32,128]{3,2,1,0:T(8,128)(2,1)S(1)} async-done(((bf16[8,3,32,128]{3,2,1,0:T(8,128)(2,1)}), bf16[8,3,32,128]{3,2,1,0:T(8,128)(2,1)S(1)}, u32[]{:S(2)}, u32[]{:S(2)}) %all-to-all-start) | async-done | bytes 196640 | tf_op jit(solution)/shard_map/all_to_all | solution.py:255
  27.0 0.7 %copy-done.16 = bf16[8,3,32,128]{3,2,1,0:T(8,128)(2,1)} copy-done((bf16[8,3,32,128]{3,2,1,0:T(8,128)(2,1)}, bf16[8,3,32,128]{3,2,1,0:T(8,128)(2,1)S(1)}, u32[]{:S(2)}) %copy-start.16) | copy-done | bytes 196632
  27.7 1.7 %chunk_scan.1 = bf16[8,3,32,128]{3,2,1,0:T(8,128)(2,1)} custom-call(bf16[8,3,32,128]{3,2,1,0:T(8,128)(2,1)} %copy-done.16, f32[32,128]{1,0:T(8,128)} %constant_dynamic-slice_fusion.rate_ref), custom_call_target="tpu_custom_call" | custom-call | tf_op jit(solution)/shard_map/chunk_scan/pallas_call | solution.py:278
  29.3 3.4 %all-to-all-start.1 = ((bf16[8,3,32,128]{3,2,1,0:T(8,128)(2,1)}), bf16[8,3,32,128]{3,2,1,0:T(8,128)(2,1)S(1)}, u32[]{:S(2)}, u32[]{:S(2)}) async-start(bf16[8,3,32,128]{3,2,1,0:T(8,128)(2,1)} %chunk_scan.1), calls=%async_computation.1 | async-start | bytes 393216 | tf_op jit(solution)/shard_map/all_to_all | solution.py:283
  32.8 0.9 %copy-done.12 = f32[2048,16]{0,1:T(8,128)S(1)} copy-done((f32[2048,16]{0,1:T(8,128)S(1)}, f32[2048,16]{0,1:T(8,128)}, u32[]{:S(2)}) %copy-start.12) | copy-done | bytes 131096
  33.7 6.3 %local_conv.1 = (f32[2,128,8,128]{3,2,1,0:T(8,128)S(1)}, f32[2,128,8,128]{3,2,1,0:T(8,128)S(1)}) custom-call(bf16[128,2048]{1,0:T(8,128)(2,1)S(1)} %copy-done.1, bf16[128,2048]{1,0:T(8,128)(2,1)S(1)} %copy-done.3, bf16[128,2048]{1,0:T(8,128)(2,1)S(1)} %copy-done.5, bf16[128,2048]{1,0:T(8,128)(2,1)S(1)} %copy-done.7, f32[16,2048]{1,0:T(8,128)S(1)} %bitcast.13, ...), custom_call_target="tpu_custom_call" | custom-call | flops 33554432 | bytes 4194304 | tf_op jit(solution)/shard_map/local_conv/pallas_call | solution.py:257
  40.0 1.0 %copy-done.10 = f32[2,128,8,128]{3,2,1,0:T(8,128)} copy-done((f32[2,128,8,128]{3,2,1,0:T(8,128)}, f32[2,128,8,128]{3,2,1,0:T(8,128)S(1)}, u32[]{:S(2)}) %copy-start.10) | copy-done | bytes 1048600
  41.0 0.7 %multiply_reduce_fusion = f32[]{:T(128)} fusion(bf16[8,3,32,128]{3,2,1,0:T(8,128)(2,1)S(1)} %all-to-all-done.1.in_ref), kind=kLoop, calls=%fused_computation.1 | loop fusion | flops 98303 | bytes 65540 | tf_op jit(solution)/shard_map/reduce_sum | solution.py:286
  41.7 1.5 %collective-permute-start = (f32[]{:T(128)}, f32[]{:T(128)}, u32[]{:S(2)}, u32[]{:S(2)}) collective-permute-start(f32[]{:T(128)} %multiply_reduce_fusion), channel_id=1, source_target_pairs={{0,1},{1,2},{2,3},{3,0},{4,5},{5,6},{6,7},{7,4},{8,9},{9,10},{10,1... | collective-permute-start | bytes 20 | tf_op jit(solution)/shard_map/ppermute | solution.py:289
  43.2 1.5 %collective-permute-start.1 = (f32[]{:T(128)}, f32[]{:T(128)}, u32[]{:S(2)}, u32[]{:S(2)}) collective-permute-start(f32[]{:T(128)} %multiply_reduce_fusion), channel_id=1, source_target_pairs={{0,2},{1,3},{2,0},{3,1},{4,6},{5,7},{6,4},{7,5},{8,10},{9,11},{10,... | collective-permute-start | bytes 20 | tf_op jit(solution)/shard_map/ppermute | solution.py:289
  44.7 1.4 %collective-permute-start.2 = (f32[]{:T(128)}, f32[]{:T(128)}, u32[]{:S(2)}, u32[]{:S(2)}) collective-permute-start(f32[]{:T(128)} %multiply_reduce_fusion), channel_id=1, source_target_pairs={{0,3},{1,0},{2,1},{3,2},{4,7},{5,4},{6,5},{7,6},{8,11},{9,8},{10,9... | collective-permute-start | bytes 20 | tf_op jit(solution)/shard_map/ppermute | solution.py:289
  46.2 1.2 %copy-done.11 = f32[2,128,8,128]{3,2,1,0:T(8,128)S(1)} copy-done((f32[2,128,8,128]{3,2,1,0:T(8,128)S(1)}, f32[2,128,8,128]{3,2,1,0:T(8,128)}, u32[]{:S(2)}) %copy-start.11) | copy-done | bytes 1048600
  47.4 0.9 %copy-done.13 = f32[2048,16]{0,1:T(8,128)S(1)} copy-done((f32[2048,16]{0,1:T(8,128)S(1)}, f32[2048,16]{0,1:T(8,128)}, u32[]{:S(2)}) %copy-start.13) | copy-done | bytes 131096
  48.3 5.1 %finish.1 = (bf16[128,2048]{1,0:T(8,128)(2,1)}, bf16[128,2048]{1,0:T(8,128)(2,1)}, bf16[128,2048]{1,0:T(8,128)(2,1)}, bf16[128,2048]{1,0:T(8,128)(2,1)}, f32[16,2048]{1,0:T(8,128)S(1)}) custom-call(bf16[128,2048]{1,0:T(8,128)(2,1)S(1)} %copy-done.1, bf16[128,2048]{1,0:T(8,128)(2,1)S(1)} %copy-done.3, bf16[128,2048]{1,0:T(8,128)(2,1)S(1)} %copy-done.5, ...), custom_call_target="tpu_custom_call" | custom-call | flops 16777216 | bytes 6291456 | tf_op jit(solution)/shard_map/finish/pallas_call | solution.py:295
  53.4 0.7 %copy-done.14 = f32[16,2048]{1,0:T(8,128)} copy-done((f32[16,2048]{1,0:T(8,128)}, f32[16,2048]{1,0:T(8,128)S(1)}, u32[]{:S(2)}) %copy-start.14) | copy-done | bytes 131096
  56.6 1.6 %multiply_bitcast_fusion = f32[2048,16]{0,1:T(8,128)} fusion(f32[16,2048]{1,0:T(8,128)} %copy-done.14, f32[]{:T(128)S(6)} %min_shard_map.3), kind=kLoop, calls=%fused_computation | loop fusion | flops 32768 | bytes 262148 | tf_op jit(solution)/shard_map/transpose | solution.py:332
  (29 shorter events, 0.1 us)
Async XLA Ops:
  0.6 1.0 %copy-start = (bf16[128,2048]{1,0:T(8,128)(2,1)S(1)}, bf16[128,2048]{1,0:T(8,128)(2,1)}, u32[]{:S(2)}) copy-start(bf16[128,2048]{1,0:T(8,128)(2,1)} %q_ref.5) | copy-start | bytes 1572868
  1.7 1.0 %copy-start.2 = (bf16[128,2048]{1,0:T(8,128)(2,1)S(1)}, bf16[128,2048]{1,0:T(8,128)(2,1)}, u32[]{:S(2)}) copy-start(bf16[128,2048]{1,0:T(8,128)(2,1)} %k_ref.5) | copy-start | bytes 1572868
  2.7 1.0 %copy-start.4 = (bf16[128,2048]{1,0:T(8,128)(2,1)S(1)}, bf16[128,2048]{1,0:T(8,128)(2,1)}, u32[]{:S(2)}) copy-start(bf16[128,2048]{1,0:T(8,128)(2,1)} %v_ref.5) | copy-start | bytes 1572868
  3.8 1.0 %copy-start.6 = (bf16[128,2048]{1,0:T(8,128)(2,1)S(1)}, bf16[128,2048]{1,0:T(8,128)(2,1)}, u32[]{:S(2)}) copy-start(bf16[128,2048]{1,0:T(8,128)(2,1)} %ct_ref.5) | copy-start | bytes 1572868
  4.8 0.9 %copy-start.8 = (f32[2048,16]{0,1:T(8,128)S(1)}, f32[2048,16]{0,1:T(8,128)}, u32[]{:S(2)}) copy-start(f32[2048,16]{0,1:T(8,128)} %param.10) | copy-start | bytes 393220
  5.7 12.9 %copy-start.9 = (f32[2048,16]{0,1:T(8,128)S(1)}, f32[2048,16]{0,1:T(8,128)}, u32[]{:S(2)}) copy-start(f32[2048,16]{0,1:T(8,128)} %param.10) | copy-start | bytes 393220
  5.7 27.0 %copy-start.7 = (bf16[128,2048]{1,0:T(8,128)(2,1)S(1)}, bf16[128,2048]{1,0:T(8,128)(2,1)}, u32[]{:S(2)}) copy-start(bf16[128,2048]{1,0:T(8,128)(2,1)} %ct_ref.5) | copy-start | bytes 1572868
  12.2 20.6 %copy-start.5 = (bf16[128,2048]{1,0:T(8,128)(2,1)S(1)}, bf16[128,2048]{1,0:T(8,128)(2,1)}, u32[]{:S(2)}) copy-start(bf16[128,2048]{1,0:T(8,128)(2,1)} %v_ref.5) | copy-start | bytes 1572868
  12.2 14.8 %all-to-all-start = ((bf16[8,3,32,128]{3,2,1,0:T(8,128)(2,1)}), bf16[8,3,32,128]{3,2,1,0:T(8,128)(2,1)S(1)}, u32[]{:S(2)}, u32[]{:S(2)}) async-start(bf16[8,3,32,128]{3,2,1,0:T(8,128)(2,1)} %chunk_states.1), calls=%async_computation | async-start | bytes 393216 | tf_op jit(solution)/shard_map/all_to_all | solution.py:255
  18.7 14.1 %copy-start.1 = (bf16[128,2048]{1,0:T(8,128)(2,1)S(1)}, bf16[128,2048]{1,0:T(8,128)(2,1)}, u32[]{:S(2)}) copy-start(bf16[128,2048]{1,0:T(8,128)(2,1)} %q_ref.5) | copy-start | bytes 1572868
  18.7 14.1 %copy-start.3 = (bf16[128,2048]{1,0:T(8,128)(2,1)S(1)}, bf16[128,2048]{1,0:T(8,128)(2,1)}, u32[]{:S(2)}) copy-start(bf16[128,2048]{1,0:T(8,128)(2,1)} %k_ref.5) | copy-start | bytes 1572868
  27.0 0.7 %copy-start.16 = (bf16[8,3,32,128]{3,2,1,0:T(8,128)(2,1)}, bf16[8,3,32,128]{3,2,1,0:T(8,128)(2,1)S(1)}, u32[]{:S(2)}) copy-start(bf16[8,3,32,128]{3,2,1,0:T(8,128)(2,1)S(1)} %all-to-all-done.in_ref) | copy-start | bytes 589828
  29.3 11.7 %all-to-all-start.1 = ((bf16[8,3,32,128]{3,2,1,0:T(8,128)(2,1)}), bf16[8,3,32,128]{3,2,1,0:T(8,128)(2,1)S(1)}, u32[]{:S(2)}, u32[]{:S(2)}) async-start(bf16[8,3,32,128]{3,2,1,0:T(8,128)(2,1)} %chunk_scan.1), calls=%async_computation.1 | async-start | bytes 393216 | tf_op jit(solution)/shard_map/all_to_all | solution.py:283
  32.8 0.9 %copy-start.12 = (f32[2048,16]{0,1:T(8,128)S(1)}, f32[2048,16]{0,1:T(8,128)}, u32[]{:S(2)}) copy-start(f32[2048,16]{0,1:T(8,128)} %param.11) | copy-start | bytes 393220
  40.0 1.0 %copy-start.10 = (f32[2,128,8,128]{3,2,1,0:T(8,128)}, f32[2,128,8,128]{3,2,1,0:T(8,128)S(1)}, u32[]{:S(2)}) copy-start(f32[2,128,8,128]{3,2,1,0:T(8,128)S(1)} %get-tuple-element.13.adj_ref) | copy-start | bytes 3145732
  41.0 5.1 %copy-start.15 = (f32[2048]{0:T(1024)S(1)}, f32[2048]{0:T(1024)}, u32[]{:S(2)}) copy-start(f32[2048]{0:T(1024)} %param.12) | copy-start | bytes 24580
  41.7 12.4 %collective-permute-start = (f32[]{:T(128)}, f32[]{:T(128)}, u32[]{:S(2)}, u32[]{:S(2)}) collective-permute-start(f32[]{:T(128)} %multiply_reduce_fusion), channel_id=1, source_target_pairs={{0,1},{1,2},{2,3},{3,0},{4,5},{5,6},{6,7},{7,4},{8,9},{9,10},{10,1... | collective-permute-start | bytes 20 | tf_op jit(solution)/shard_map/ppermute | solution.py:289
  43.2 12.1 %collective-permute-start.1 = (f32[]{:T(128)}, f32[]{:T(128)}, u32[]{:S(2)}, u32[]{:S(2)}) collective-permute-start(f32[]{:T(128)} %multiply_reduce_fusion), channel_id=1, source_target_pairs={{0,2},{1,3},{2,0},{3,1},{4,6},{5,7},{6,4},{7,5},{8,10},{9,11},{10,... | collective-permute-start | bytes 20 | tf_op jit(solution)/shard_map/ppermute | solution.py:289
  44.7 11.2 %collective-permute-start.2 = (f32[]{:T(128)}, f32[]{:T(128)}, u32[]{:S(2)}, u32[]{:S(2)}) collective-permute-start(f32[]{:T(128)} %multiply_reduce_fusion), channel_id=1, source_target_pairs={{0,3},{1,0},{2,1},{3,2},{4,7},{5,4},{6,5},{7,6},{8,11},{9,8},{10,9... | collective-permute-start | bytes 20 | tf_op jit(solution)/shard_map/ppermute | solution.py:289
  46.1 1.2 %copy-start.11 = (f32[2,128,8,128]{3,2,1,0:T(8,128)S(1)}, f32[2,128,8,128]{3,2,1,0:T(8,128)}, u32[]{:S(2)}) copy-start(f32[2,128,8,128]{3,2,1,0:T(8,128)} %copy-done.10) | copy-start | bytes 3145732
  47.4 0.9 %copy-start.13 = (f32[2048,16]{0,1:T(8,128)S(1)}, f32[2048,16]{0,1:T(8,128)}, u32[]{:S(2)}) copy-start(f32[2048,16]{0,1:T(8,128)} %param.11) | copy-start | bytes 393220
  53.4 0.7 %copy-start.14 = (f32[16,2048]{1,0:T(8,128)}, f32[16,2048]{1,0:T(8,128)S(1)}, u32[]{:S(2)}) copy-start(f32[16,2048]{1,0:T(8,128)S(1)} %get-tuple-element.18) | copy-start | bytes 393220

commit v2 on v1

--- a/solution.py
+++ b/solution.py
@@ -1,3 +1,4 @@
+from functools import partial
 import math
 
 import jax
@@ -11,7 +12,7 @@
 WIRE = jnp.bfloat16
 LANES = 128
 UNROLL = 8
-VMEM_LIMIT = 40 * 1024 * 1024
+VMEM_LIMIT = 60 * 1024 * 1024
 
 
 def gate(left_ref, right_ref, cols):
@@ -46,12 +47,13 @@
         pulled[s * seq : (s + 1) * seq, :] = gate(ct_ref, q_ref, cols)
 
 
-def states_kernel(q_ref, k_ref, v_ref, ct_ref, rate_ref, out_ref, gated, pulled, table, states):
+def states_kernel(q_ref, k_ref, v_ref, ct_ref, rate_ref, out_ref, token_ref, gated, pulled, table, states):
     seq = q_ref.shape[0]
     modes = rate_ref.shape[0]
     sub = q_ref.shape[1] // LANES
     fill_lines(k_ref, v_ref, q_ref, ct_ref, gated, pulled, sub, seq)
     decay = [jnp.exp(-r) for r in spread(rate_ref, modes, sub, table)]
+    token_ref[...] = jnp.zeros_like(token_ref)
     zeros = tuple(jnp.zeros((sub, LANES), F32) for _ in range(modes))
 
     def forward(i, carry):
@@ -88,41 +90,41 @@
 
 
 def local_kernel(
-    q_ref, k_ref, v_ref, ct_ref, rate_ref, res_ref, conv_ref, adj_ref, gated, pulled, table
+    reverse, left_ref, right_ref, rate_ref, res_ref, after_ref, out_ref, token_ref, lines, table
 ):
-    seq = q_ref.shape[0]
+    token_ref[...] = jnp.zeros_like(token_ref)
+    seq = left_ref.shape[0]
     modes = rate_ref.shape[0]
-    sub = q_ref.shape[1] // LANES
-    fill_lines(k_ref, v_ref, q_ref, ct_ref, gated, pulled, sub, seq)
+    sub = left_ref.shape[1] // LANES
+    for s in range(sub):
+        cols = slice(s * LANES, (s + 1) * LANES)
+        lines[s * seq : (s + 1) * seq, :] = gate(left_ref, right_ref, cols)
     rates = spread(rate_ref, modes, sub, table)
     weights = spread(res_ref, modes, sub, table)
     decay = [jnp.exp(-r) for r in rates]
     coef = [w * jnp.sqrt(1.0 - jnp.exp(-2.0 * r)) for w, r in zip(weights, rates)]
+
+    def body(i, carry):
+        held = list(carry)
+        for u in range(UNROLL):
+            t = i * UNROLL + u
+            if reverse:
+                t = seq - 1 - t
+            x = rows_of(lines, t, sub, seq)
+            total = [None] * 4
+            for n in range(modes):
+                held[n] = decay[n] * held[n] + x
+                term = coef[n] * held[n]
+                total[n % 4] = term if total[n % 4] is None else total[n % 4] + term
+            out_ref[0, t] = tree_sum(total)
+        return tuple(held)
+
     zeros = tuple(jnp.zeros((sub, LANES), F32) for _ in range(modes))
-
-    def scan(source, target, reverse):
-        def body(i, carry):
-            held = list(carry)
-            for u in range(UNROLL):
-                t = i * UNROLL + u
-                if reverse:
-                    t = seq - 1 - t
-                x = rows_of(source, t, sub, seq)
-                total = [None] * 4
-                for n in range(modes):
-                    held[n] = decay[n] * held[n] + x
-                    term = coef[n] * held[n]
-                    total[n % 4] = term if total[n % 4] is None else total[n % 4] + term
-                target[0, t] = tree_sum(total)
-            return tuple(held)
-
-        lax.fori_loop(0, seq // UNROLL, body, zeros)
-
-    scan(gated, conv_ref, False)
-    scan(pulled, adj_ref, True)
-
-
-def chunks_kernel(in_ref, rate_ref, out_ref):
+    lax.fori_loop(0, seq // UNROLL, body, zeros)
+
+
+def chunks_kernel(in_ref, rate_ref, after_ref, out_ref, token_ref):
+    token_ref[...] = jnp.zeros_like(token_ref)
     count = in_ref.shape[0]
     rate = rate_ref[...]
     step = jnp.exp(-rate)
@@ -237,14 +239,16 @@
     lines_scratch = pltpu.VMEM((sub * seq, LANES), F32)
     table_scratch = pltpu.VMEM((block_rows, LANES), F32)
     states_scratch = pltpu.VMEM((3, block_rows, LANES), F32)
+    token_spec = pl.BlockSpec((8, LANES), lambda b: (0, 0))
+    token_shape = jax.ShapeDtypeStruct((8, LANES), F32)
     elements = seq * channels * modes
 
-    packed = pl.pallas_call(
+    packed, token = pl.pallas_call(
         states_kernel,
         grid=(blocks,),
         in_specs=[line_spec] * 4 + [table_spec],
-        out_specs=pack_spec,
-        out_shape=jax.ShapeDtypeStruct((ctx, 3, slab, LANES), WIRE),
+        out_specs=[pack_spec, token_spec],
+        out_shape=[jax.ShapeDtypeStruct((ctx, 3, slab, LANES), WIRE), token_shape],
         scratch_shapes=[lines_scratch, lines_scratch, table_scratch, states_scratch],
         compiler_params=params,
         cost_estimate=pl.CostEstimate(
@@ -254,20 +258,22 @@
     )(queries, keys_in, values_in, cotangent, rates)
     gathered = lax.all_to_all(packed, "ctx", split_axis=0, concat_axis=0, tiled=True)
 
-    conv, adj = pl.pallas_call(
-        local_kernel,
-        grid=(blocks,),
-        in_specs=[line_spec] * 4 + [table_spec] * 2,
-        out_specs=[tall_spec] * 2,
-        out_shape=[jax.ShapeDtypeStruct((blocks, seq, sub, LANES), F32)] * 2,
-        scratch_shapes=[lines_scratch, lines_scratch, table_scratch],
-        compiler_params=params,
-        cost_estimate=pl.CostEstimate(
-            flops=8 * elements, bytes_accessed=16 * seq * channels, transcendentals=0
-        ),
-        name="local_conv",
-    )(queries, keys_in, values_in, cotangent, rates, weights)
-
+    def local(reverse, left, right, after, name):
+        return pl.pallas_call(
+            partial(local_kernel, reverse),
+            grid=(blocks,),
+            in_specs=[line_spec] * 2 + [table_spec] * 2 + [pl.BlockSpec(memory_space=pl.ANY)],
+            out_specs=[tall_spec, token_spec],
+            out_shape=[jax.ShapeDtypeStruct((blocks, seq, sub, LANES), F32), token_shape],
+            scratch_shapes=[lines_scratch, table_scratch],
+            compiler_params=params,
+            cost_estimate=pl.CostEstimate(
+                flops=4 * elements, bytes_accessed=8 * seq * channels, transcendentals=0
+            ),
+            name=name,
+        )(left, right, rates, weights, after)
+
+    conv, token = local(False, keys_in, values_in, token, "local_conv")
     own_rates = lax.dynamic_slice_in_dim(
         rates.reshape(modes, blocks, sub, LANES).transpose(1, 0, 2, 3).reshape(-1, LANES),
         lax.axis_index("ctx") * slab,
@@ -275,11 +281,14 @@
         0,
     )
     CHUNK[0] = seq
-    carries = pl.pallas_call(
+    carries, token = pl.pallas_call(
         chunks_kernel,
-        out_shape=jax.ShapeDtypeStruct((ctx, 3, slab, LANES), WIRE),
+        out_shape=[jax.ShapeDtypeStruct((ctx, 3, slab, LANES), WIRE), token_shape],
+        in_specs=[pl.BlockSpec(), pl.BlockSpec(), pl.BlockSpec(memory_space=pl.ANY)],
+        compiler_params=pltpu.CompilerParams(vmem_limit_bytes=4 * 1024 * 1024),
         name="chunk_scan",
-    )(gathered, own_rates)
+    )(gathered, own_rates, token)
+    adj, _ = local(True, cotangent, queries, token, "local_adjoint")
     carried = lax.all_to_all(carries, "ctx", split_axis=0, concat_axis=0, tiled=True)
 
     raw_rows = carried[:, 2].astype(F32)

time: 58.9 us -> 52.2 us (0.89)
  local copies, waits for them, and re-layouts: 11.1 us -> 0.64 us
  Pallas kernels: 19.6 us -> 24.8 us
  waiting for transfers between devices: 7.65 us -> 6.51 us
    unnamed x35 -> x9, local copies, waits for them, and re-layouts: 10.5 us -> 0.63 us
    all_to_all x1, waiting for transfers between devices: 7.64 us -> 3.28 us  [shards(): lax.all_to_all(packed, 'ctx', split_axis=0, concat_axis=0, tiled=True)]
    all_to_all x1, waiting for transfers between devices: 0.01 us -> 3.23 us  [shards(): lax.all_to_all(carries, 'ctx', split_axis=0, concat_axis=0, tiled=True)]
    pallas_call x2 -> x3, Pallas kernels: 7.99 us -> 10.8 us  [the longest x2 10 us: local(): pl.pallas_call(partial(local_kernel, reverse), grid=(blocks,), in_specs=[...]
    pallas_call x1, Pallas kernels: 5.13 us -> 6.55 us  [shards(): pl.pallas_call(finish_kernel, grid=(blocks,), in_specs=[line_spec] * 4 +...]
    pallas_call x1, Pallas kernels: 6.48 us -> 7.53 us  [shards(): pl.pallas_call(states_kernel, grid=(blocks,), in_specs=[line_spec] * 4 +...]
    dynamic_slice x1, local copies, waits for them, and re-layouts: 0.61 us -> 0.01 us  [shards(): lax.dynamic_slice_in_dim(rates.reshape(modes, blocks, sub, LANES).transpo...]
  transfers between devices with their start and end apart: 5 -> 5, of which waited for: 1 -> 2; matrix products, arithmetic and copies ran while one was open for 1% -> 0% of each run, Pallas kernels for 20% -> 32%
where the time goes in v2:
time: 52.2 us; the launch traced here: 51.8 us
  Pallas kernels  24.8 us (48%)
  starting transfers between devices  14.3 us (27%)
  waiting for transfers between devices  6.51 us (12%)
  between operations  3.24 us (6%)
  other arithmetic  2.23 us (4%)
  local copies, waits for them, and re-layouts  0.64 us (1%)
    pallas_call x2, Pallas kernels, local(): pl.pallas_call(partial(local_kernel, reverse), grid=(blocks,), in_specs=[...  10 us
    pallas_call x1, Pallas kernels, shards(): pl.pallas_call(states_kernel, grid=(blocks,), in_specs=[line_spec] * 4 +...  7.53 us
    pallas_call x1, Pallas kernels, shards(): pl.pallas_call(finish_kernel, grid=(blocks,), in_specs=[line_spec] * 4 +...  6.55 us
    all_to_all x1, starting transfers between devices, shards(): lax.all_to_all(packed, 'ctx', split_axis=0, concat_axis=0, tiled=True)  6.46 us
    ppermute x3, starting transfers between devices, shards(): lax.ppermute(square, 'tp', [(i, (i + hop) % tp) for i in range(tp)])  4.44 us
    all_to_all x1, starting transfers between devices, shards(): lax.all_to_all(carries, 'ctx', split_axis=0, concat_axis=0, tiled=True)  3.39 us
    all_to_all x1, waiting for transfers between devices, shards(): lax.all_to_all(packed, 'ctx', split_axis=0, concat_axis=0, tiled=True)  3.28 us
    all_to_all x1, waiting for transfers between devices, shards(): lax.all_to_all(carries, 'ctx', split_axis=0, concat_axis=0, tiled=True)  3.23 us
  transfers between devices with their start and end apart: 5, of which 2 were waited for; matrix products, arithmetic and copies ran while one was open for 0% of the time, Pallas kernels for 32%

profile of v2, /device:TPU:0, one launch (start us, length us, event | category | flops | bytes accessed | tf_op | source)
XLA Modules:
  0.0 51.8 jit_solution(2489302911815933639)
XLA Ops:
  0.6 7.5 %chunk_states.1 = (bf16[8,3,32,128]{3,2,1,0:T(8,128)(2,1)}, f32[8,128]{1,0:T(8,128)}) custom-call(bf16[128,2048]{1,0:T(8,128)(2,1)} %q_ref.3, bf16[128,2048]{1,0:T(8,128)(2,1)} %k_ref.3, bf16[128,2048]{1,0:T(8,128)(2,1)} %v_ref.3, bf16[128,2048]{1,0:T(8,128)(2,1)} %ct_ref.3, f32[16,2048]{1,0:T(8,128)} %bitcast.11), custom_call_target="tpu_custom_call" | custom-call | flops 25165824 | bytes 2097152 | tf_op jit(solution)/shard_map/chunk_states/pallas_call | solution.py:246
  8.2 0.0 copy-start.2
  8.2 6.5 %all-to-all-start = ((bf16[8,3,32,128]{3,2,1,0:T(8,128)(2,1)}), bf16[8,3,32,128]{3,2,1,0:T(8,128)(2,1)S(1)}, u32[]{:S(2)}, u32[]{:S(2)}) async-start(bf16[8,3,32,128]{3,2,1,0:T(8,128)(2,1)} %get-tuple-element.19), calls=%async_computation | async-start | bytes 393216 | tf_op jit(solution)/shard_map/all_to_all | solution.py:259
  14.6 0.0 copy-done.2
  14.7 5.0 %local_conv.1 = (f32[2,128,8,128]{3,2,1,0:T(8,128)}, f32[8,128]{1,0:T(8,128)}) custom-call(bf16[128,2048]{1,0:T(8,128)(2,1)} %k_ref.3, bf16[128,2048]{1,0:T(8,128)(2,1)} %v_ref.3, f32[16,2048]{1,0:T(8,128)} %bitcast.12, f32[16,2048]{1,0:T(8,128)} %bitcast.16, f32[8,128]{1,0:T(8,128)} %get-tuple-element.17.after_ref), custom_call_target="tpu_custom_call" | custom-call | flops 16777216 | bytes 2097152 | tf_op jit(solution)/shard_map/local_conv/pallas_call | solution.py:262
  19.7 0.0 copy-start.1
  19.7 3.3 %all-to-all-done.in_ref = bf16[8,3,32,128]{3,2,1,0:T(8,128)(2,1)S(1)} async-done(((bf16[8,3,32,128]{3,2,1,0:T(8,128)(2,1)}), bf16[8,3,32,128]{3,2,1,0:T(8,128)(2,1)S(1)}, u32[]{:S(2)}, u32[]{:S(2)}) %all-to-all-start) | async-done | bytes 196640 | tf_op jit(solution)/shard_map/all_to_all | solution.py:259
  23.0 0.0 copy-done.1
  23.0 0.7 %chunk_scan.1 = (bf16[8,3,32,128]{3,2,1,0:T(8,128)(2,1)}, f32[8,128]{1,0:T(8,128)S(1)}) custom-call(bf16[8,3,32,128]{3,2,1,0:T(8,128)(2,1)S(1)} %all-to-all-done.in_ref, f32[32,128]{1,0:T(8,128)S(1)} %constant_dynamic-slice_fusion.rate_ref, f32[8,128]{1,0:T(8,128)S(1)} %copy-done.1), custom_call_target="tpu_custom_call" | custom-call | tf_op jit(solution)/shard_map/chunk_scan/pallas_call | solution.py:284
  23.7 0.0 copy-start
  23.7 0.6 %copy-done = f32[8,128]{1,0:T(8,128)} copy-done((f32[8,128]{1,0:T(8,128)}, f32[8,128]{1,0:T(8,128)S(1)}, u32[]{:S(2)}) %copy-start) | copy-done | bytes 4120
  24.3 3.4 %all-to-all-start.1 = ((bf16[8,3,32,128]{3,2,1,0:T(8,128)(2,1)}), bf16[8,3,32,128]{3,2,1,0:T(8,128)(2,1)S(1)}, u32[]{:S(2)}, u32[]{:S(2)}) async-start(bf16[8,3,32,128]{3,2,1,0:T(8,128)(2,1)} %get-tuple-element.23), calls=%async_computation.1 | async-start | bytes 393216 | tf_op jit(solution)/shard_map/all_to_all | solution.py:292
  27.7 5.0 %local_adjoint.1 = (f32[2,128,8,128]{3,2,1,0:T(8,128)}, f32[8,128]{1,0:T(8,128)}) custom-call(bf16[128,2048]{1,0:T(8,128)(2,1)} %ct_ref.3, bf16[128,2048]{1,0:T(8,128)(2,1)} %q_ref.3, f32[16,2048]{1,0:T(8,128)} %bitcast.13, f32[16,2048]{1,0:T(8,128)} %bitcast.17, f32[8,128]{1,0:T(8,128)} %copy-done), custom_call_target="tpu_custom_call" | custom-call | flops 16777216 | bytes 2097152 | tf_op jit(solution)/shard_map/local_adjoint/pallas_call | solution.py:262
  32.7 3.2 %all-to-all-done.1.in_ref = bf16[8,3,32,128]{3,2,1,0:T(8,128)(2,1)S(1)} async-done(((bf16[8,3,32,128]{3,2,1,0:T(8,128)(2,1)}), bf16[8,3,32,128]{3,2,1,0:T(8,128)(2,1)S(1)}, u32[]{:S(2)}, u32[]{:S(2)}) %all-to-all-start.1) | async-done | bytes 196640 | tf_op jit(solution)/shard_map/all_to_all | solution.py:292
  36.0 0.7 %multiply_reduce_fusion = f32[]{:T(128)} fusion(bf16[8,3,32,128]{3,2,1,0:T(8,128)(2,1)S(1)} %all-to-all-done.1.in_ref), kind=kLoop, calls=%fused_computation.1 | loop fusion | flops 98303 | bytes 65540 | tf_op jit(solution)/shard_map/reduce_sum | solution.py:295
  36.6 1.5 %collective-permute-start = (f32[]{:T(128)}, f32[]{:T(128)}, u32[]{:S(2)}, u32[]{:S(2)}) collective-permute-start(f32[]{:T(128)} %multiply_reduce_fusion), channel_id=1, source_target_pairs={{0,1},{1,2},{2,3},{3,0},{4,5},{5,6},{6,7},{7,4},{8,9},{9,10},{10,1... | collective-permute-start | bytes 20 | tf_op jit(solution)/shard_map/ppermute | solution.py:298
  38.1 1.5 %collective-permute-start.1 = (f32[]{:T(128)}, f32[]{:T(128)}, u32[]{:S(2)}, u32[]{:S(2)}) collective-permute-start(f32[]{:T(128)} %multiply_reduce_fusion), channel_id=1, source_target_pairs={{0,2},{1,3},{2,0},{3,1},{4,6},{5,7},{6,4},{7,5},{8,10},{9,11},{10,... | collective-permute-start | bytes 20 | tf_op jit(solution)/shard_map/ppermute | solution.py:298
  39.6 1.4 %collective-permute-start.2 = (f32[]{:T(128)}, f32[]{:T(128)}, u32[]{:S(2)}, u32[]{:S(2)}) collective-permute-start(f32[]{:T(128)} %multiply_reduce_fusion), channel_id=1, source_target_pairs={{0,3},{1,0},{2,1},{3,2},{4,7},{5,4},{6,5},{7,6},{8,11},{9,8},{10,9... | collective-permute-start | bytes 20 | tf_op jit(solution)/shard_map/ppermute | solution.py:298
  41.1 0.0 copy-done.3
  41.1 6.6 %finish.1 = (bf16[128,2048]{1,0:T(8,128)(2,1)}, bf16[128,2048]{1,0:T(8,128)(2,1)}, bf16[128,2048]{1,0:T(8,128)(2,1)}, bf16[128,2048]{1,0:T(8,128)(2,1)}, f32[16,2048]{1,0:T(8,128)}) custom-call(bf16[128,2048]{1,0:T(8,128)(2,1)} %q_ref.3, bf16[128,2048]{1,0:T(8,128)(2,1)} %k_ref.3, bf16[128,2048]{1,0:T(8,128)(2,1)} %v_ref.3, bf16[128,2048]{1,0:T(8,128)(2,1)} %ct_ref.3, ...), custom_call_target="tpu_custom_call" | custom-call | flops 16777216 | bytes 6291456 | tf_op jit(solution)/shard_map/finish/pallas_call | solution.py:304
  47.6 0.0 collective-permute-done
  48.9 0.0 collective-permute-done.1
  49.5 0.0 collective-permute-done.2
  50.2 1.6 %multiply_bitcast_fusion = f32[2048,16]{0,1:T(8,128)} fusion(f32[16,2048]{1,0:T(8,128)} %get-tuple-element.28, f32[]{:T(128)S(6)} %min_shard_map.3), kind=kLoop, calls=%fused_computation | loop fusion | flops 32768 | bytes 262148 | tf_op jit(solution)/shard_map/transpose | solution.py:341
  (4 shorter events, 0.0 us)
Async XLA Ops:
  8.2 6.5 %copy-start.2 = (f32[2048,16]{0,1:T(8,128)S(1)}, f32[2048,16]{0,1:T(8,128)}, u32[]{:S(2)}) copy-start(f32[2048,16]{0,1:T(8,128)} %param.10) | copy-start | bytes 393220
  8.2 14.8 %all-to-all-start = ((bf16[8,3,32,128]{3,2,1,0:T(8,128)(2,1)}), bf16[8,3,32,128]{3,2,1,0:T(8,128)(2,1)S(1)}, u32[]{:S(2)}, u32[]{:S(2)}) async-start(bf16[8,3,32,128]{3,2,1,0:T(8,128)(2,1)} %get-tuple-element.19), calls=%async_computation | async-start | bytes 393216 | tf_op jit(solution)/shard_map/all_to_all | solution.py:259
  19.7 3.3 %copy-start.1 = (f32[8,128]{1,0:T(8,128)S(1)}, f32[8,128]{1,0:T(8,128)}, u32[]{:S(2)}) copy-start(f32[8,128]{1,0:T(8,128)} %get-tuple-element.20.after_ref) | copy-start | bytes 12292
  23.7 0.6 %copy-start = (f32[8,128]{1,0:T(8,128)}, f32[8,128]{1,0:T(8,128)S(1)}, u32[]{:S(2)}) copy-start(f32[8,128]{1,0:T(8,128)S(1)} %get-tuple-element.21.after_ref) | copy-start | bytes 12292
  24.3 11.7 %all-to-all-start.1 = ((bf16[8,3,32,128]{3,2,1,0:T(8,128)(2,1)}), bf16[8,3,32,128]{3,2,1,0:T(8,128)(2,1)S(1)}, u32[]{:S(2)}, u32[]{:S(2)}) async-start(bf16[8,3,32,128]{3,2,1,0:T(8,128)(2,1)} %get-tuple-element.23), calls=%async_computation.1 | async-start | bytes 393216 | tf_op jit(solution)/shard_map/all_to_all | solution.py:292
  36.0 5.1 %copy-start.3 = (bf16[8,3,32,128]{3,2,1,0:T(8,128)(2,1)}, bf16[8,3,32,128]{3,2,1,0:T(8,128)(2,1)S(1)}, u32[]{:S(2)}) copy-start(bf16[8,3,32,128]{3,2,1,0:T(8,128)(2,1)S(1)} %all-to-all-done.1.in_ref) | copy-start | bytes 589828
  36.6 11.0 %collective-permute-start = (f32[]{:T(128)}, f32[]{:T(128)}, u32[]{:S(2)}, u32[]{:S(2)}) collective-permute-start(f32[]{:T(128)} %multiply_reduce_fusion), channel_id=1, source_target_pairs={{0,1},{1,2},{2,3},{3,0},{4,5},{5,6},{6,7},{7,4},{8,9},{9,10},{10,1... | collective-permute-start | bytes 20 | tf_op jit(solution)/shard_map/ppermute | solution.py:298
  38.1 10.8 %collective-permute-start.1 = (f32[]{:T(128)}, f32[]{:T(128)}, u32[]{:S(2)}, u32[]{:S(2)}) collective-permute-start(f32[]{:T(128)} %multiply_reduce_fusion), channel_id=1, source_target_pairs={{0,2},{1,3},{2,0},{3,1},{4,6},{5,7},{6,4},{7,5},{8,10},{9,11},{10,... | collective-permute-start | bytes 20 | tf_op jit(solution)/shard_map/ppermute | solution.py:298
  39.6 9.9 %collective-permute-start.2 = (f32[]{:T(128)}, f32[]{:T(128)}, u32[]{:S(2)}, u32[]{:S(2)}) collective-permute-start(f32[]{:T(128)} %multiply_reduce_fusion), channel_id=1, source_target_pairs={{0,3},{1,0},{2,1},{3,2},{4,7},{5,4},{6,5},{7,6},{8,11},{9,8},{10,9... | collective-permute-start | bytes 20 | tf_op jit(solution)/shard_map/ppermute | solution.py:298
